TPU v7x, 256 devices: a whole 4x4x8 slice. The times are simulated.
256 devices in a mesh: ctx: 16 (over x_hi, y, core), tp: 16 (over z, x_lo).
Axes of the slice: x: 4 (x_hi: 2, x_lo: 2; x = x_hi * 2 + x_lo), y: 4, z: 8, core: 2. Of those that a mesh axis runs over, the one named last changes fastest.
Arguments:
- queries: bfloat16 [8192, 8192], P('ctx', 'tp'), may hold values from -6 to 6
- keys: bfloat16 [8192, 8192], P('ctx', 'tp'), may hold values from -6 to 6
- values: bfloat16 [8192, 8192], P('ctx', 'tp'), may hold values from -10 to 10
- doc_ids: int32 [8192], P('ctx'), may hold values from 0 to 2, never falling along the last dimension, each value on 1 to 5120 neighbouring positions
- attn_gain: float32 [8192], P('tp'), may hold values from 0.5 to 1.5
Outputs:
- blended: bfloat16 [8192, 8192], P('ctx', 'tp')
Inputs may be any that keep to these rules, and one draw needn't show every extreme that they name: doc_ids never falls along the sequence; there are three documents, each of 1 to 5120 tokens, one of exactly 5120.
All inputs are finite; a program needn't handle non-finite values.
Results may differ from a plain program's by a relative error of at most 0.0095.
Values may be sent and summed in bfloat16 or wider, within the bound.
A program may use at most 128 MiB of HBM per device.

v0:
```python
import math

import jax
import jax.numpy as jnp
from jax import lax
from jax.sharding import PartitionSpec as P

D = 8192
HEAD_DIM = 128


epsilon = 1e-06
very_low = -1e30


def absorb(carry_state, query_set, key_grid, value_grid, key_docs, score_scale):
    query_rows, query_pos, query_doc = query_set
    head_count = query_rows.shape[1]
    head_size = query_rows.shape[2]
    piece_rows = key_grid.shape[0]
    block_rows = math.gcd(piece_rows, 512)
    block_count = piece_rows // block_rows
    key_tiles = key_grid.reshape(block_count, block_rows, head_count, head_size)
    value_tiles = value_grid.reshape(block_count, block_rows, head_count, head_size)
    doc_tiles = key_docs.reshape(block_count, block_rows)
    tile_starts = jnp.arange(block_count, dtype=jnp.int32) * block_rows
    last_pos = jnp.max(query_pos)
    doc_lowest = jnp.min(query_doc)
    doc_highest = jnp.max(query_doc)

    def visit(running, key_block):
        key_tile, value_tile, doc_tile, tile_start = key_block
        key_pos = tile_start + jnp.arange(block_rows, dtype=jnp.int32)
        is_live = (
            (key_pos[0] <= last_pos) & (doc_tile[0] <= doc_highest) & (doc_tile[-1] >= doc_lowest)
        )

        def attend(inner):
            row_top, summed, gathered = inner
            scores = (
                jnp.einsum("rhd,shd->hrs", query_rows, key_tile, preferred_element_type=jnp.float32)
                * score_scale
            )
            allowed = (key_pos[None, :] <= query_pos[:, None]) & (
                doc_tile[None, :] == query_doc[:, None]
            )
            scores = jnp.where(allowed[None], scores, very_low)
            new_top = jnp.maximum(row_top, jnp.max(scores, axis=2))
            weights = jnp.where(allowed[None], jnp.exp(scores - new_top[:, :, None]), 0.0)
            factor = jnp.exp(row_top - new_top)
            summed = summed * factor + jnp.sum(weights, axis=2)
            update = jnp.einsum(
                "hrs,shd->rhd",
                weights.astype(jnp.bfloat16),
                value_tile,
                preferred_element_type=jnp.float32,
            )
            gathered = gathered * jnp.transpose(factor)[:, :, None] + update
            return (new_top, summed, gathered)

        def unchanged(inner):
            return inner

        return (lax.cond(is_live, attend, unchanged, running), None)

    carry_state, _ = lax.scan(visit, carry_state, (key_tiles, value_tiles, doc_tiles, tile_starts))
    return carry_state


def finish(carry_state, row_count):
    row_top, summed, gathered = carry_state
    return (gathered / jnp.transpose(summed)[:, :, None]).reshape(row_count, -1)


def local(queries, keys, values, doc_ids, attn_gain):
    tok_rows = queries.shape[0]
    half_rows = tok_rows // 2
    channels = queries.shape[1]
    head_count = channels // HEAD_DIM
    score_scale = 1.0 / math.sqrt(HEAD_DIM)
    my_index = lax.axis_index("ctx")
    query_grid = queries.reshape(tok_rows, head_count, HEAD_DIM)
    first_q = query_grid[:half_rows]
    second_q = query_grid[half_rows:]
    first_doc = doc_ids[:half_rows]
    second_doc = doc_ids[half_rows:]
    half_offsets = jnp.arange(half_rows, dtype=jnp.int32)

    def empty_state():
        return (
            jnp.full((head_count, half_rows), very_low, jnp.float32),
            jnp.zeros((head_count, half_rows), jnp.float32),
            jnp.zeros((half_rows, head_count, HEAD_DIM), jnp.float32),
        )

    first_pos = my_index * tok_rows + half_offsets
    second_pos = my_index * tok_rows + half_rows + half_offsets
    key_piece = lax.all_gather(keys, "ctx", axis=0, tiled=True)
    value_piece = lax.all_gather(values, "ctx", axis=0, tiled=True)
    doc_piece = lax.all_gather(doc_ids, "ctx", axis=0, tiled=True)
    piece_rows = key_piece.shape[0]
    key_piece = key_piece.reshape(piece_rows, head_count, HEAD_DIM)
    value_piece = value_piece.reshape(piece_rows, head_count, HEAD_DIM)
    state_one = absorb(
        empty_state(),
        (first_q, first_pos, first_doc),
        key_piece,
        value_piece,
        doc_piece,
        score_scale,
    )
    state_two = absorb(
        empty_state(),
        (second_q, second_pos, second_doc),
        key_piece,
        value_piece,
        doc_piece,
        score_scale,
    )
    first_out = finish(state_one, half_rows)
    second_out = finish(state_two, half_rows)
    attention = jnp.concatenate([first_out, second_out], axis=0)
    attn_sq = lax.psum(jnp.sum(attention * attention, axis=1), "tp")
    attn_factor = lax.rsqrt(attn_sq / D + epsilon)
    blended = attn_gain[None, :] * attention * attn_factor[:, None]
    return blended.astype(jnp.bfloat16)


def solution(mesh):
    placed = (P("ctx", "tp"), P("ctx", "tp"), P("ctx", "tp"), P("ctx"), P("tp"))
    return jax.shard_map(
        local, mesh=mesh, in_specs=placed, out_specs=P("ctx", "tp"), check_vma=False
    )
```

profile of v0, /device:TPU:4, one launch (start us, length us, event | category | flops | bytes accessed | tf_op | source)
XLA Modules:
  0.0 515.1 jit_solution(9020274795244557614)
XLA Ops:
  8.6 22.3 %all-gather = s32[16,1,512]{2,1,0:T(1,128)S(1)} all-gather(s32[1,1,512]{2,1,0:T(1,128)} %bitcast.103), channel_id=1, replica_groups=mesh['ctx'=16,'tp'=16] {'ctx'}, dimensions={0}, use_global_device_ids=true | all-gather | bytes 34816 | tf_op jit(solution)/shard_map/all_gather | solution.py:100
  33.4 55.3 %all-gather.4.cloned.1.call-done = bf16[8192,512]{1,0:T(8,128)(2,1)} async-done(((bf16[512,512]{1,0:T(8,128)(2,1)}), bf16[8192,512]{1,0:T(8,128)(2,1)}) %all-gather.4.cloned.1.call-update) | async-done | bytes 8388624 | tf_op jit(solution)/shard_map/all_gather | solution.py:98
  88.7 12.5 %reshape.155 = bf16[16,512,4,128]{3,2,1,0:T(4,128)(2,1)} reshape(bf16[8192,512]{1,0:T(8,128)(2,1)} %all-gather.4.cloned.1.call-done) | data formatting | bytes 16777216 | tf_op jit(solution)/shard_map/reshape;reshape | solution.py:23
  101.2 9.1 %copy.29 = bf16[16,512,4,128]{3,1,2,0:T(8,128)(2,1)} copy(bf16[16,512,4,128]{3,2,1,0:T(4,128)(2,1)} %reshape.155) | data formatting | bytes 16777216
  110.3 57.0 %all-gather.6.cloned.1.call-done = bf16[8192,512]{1,0:T(8,128)(2,1)} async-done(((bf16[512,512]{1,0:T(8,128)(2,1)}), bf16[8192,512]{1,0:T(8,128)(2,1)}) %all-gather.6.cloned.1.call-update) | async-done | bytes 8388624 | tf_op jit(solution)/shard_map/all_gather | solution.py:99
  167.3 12.5 %reshape.156 = bf16[16,512,4,128]{3,2,1,0:T(4,128)(2,1)} reshape(bf16[8192,512]{1,0:T(8,128)(2,1)} %all-gather.6.cloned.1.call-done) | data formatting | bytes 16777216 | tf_op jit(solution)/shard_map/reshape;reshape | solution.py:24
  179.9 8.9 %copy.31 = bf16[16,512,4,128]{3,1,2,0:T(8,128)(2,1)} copy(bf16[16,512,4,128]{3,2,1,0:T(4,128)(2,1)} %reshape.156) | data formatting | bytes 16777216
  188.8 141.5 %while.31 = (s32[]{:T(128)}, f32[4,256]{1,0:T(4,128)S(1)}, f32[4,256]{1,0:T(4,128)S(1)}, f32[256,4,128]{2,0,1:T(8,128)S(1)}, s32[16]{0:T(128)S(1)}, /*index=5*/s...) while((s32[]{:T(128)}, f32[4,256]{1,0:T(4,128)S(1)}, ...), condition=%wide.region_17.18_spmd.clone, body=%wide.region_12.17_spmd.clone.sunk | while | flops 275910400 | bytes 9257383 | solution.py:66
  195.1 4.4 conditional.7
  196.9 2.0 fusion.27
  205.9 4.4 conditional.7
  216.6 4.4 conditional.7
  227.4 4.4 conditional.7
  229.2 2.0 fusion.27
  238.1 4.4 conditional.7
  239.9 2.0 fusion.27
  248.9 4.4 conditional.7
  259.6 4.4 conditional.7
  270.4 4.4 conditional.7
  272.2 2.0 fusion.27
  281.2 4.4 conditional.7
  330.4 140.9 %while.30 = (s32[]{:T(128)}, f32[4,256]{1,0:T(4,128)S(1)}, f32[4,256]{1,0:T(4,128)S(1)}, f32[256,4,128]{2,0,1:T(8,128)S(1)}, s32[16]{0:T(128)S(1)}, /*index=5*/s...) while((s32[]{:T(128)}, f32[4,256]{1,0:T(4,128)S(1)}, ...), condition=%wide.region_8.9_spmd.clone, body=%wide.region_3.8_spmd.clone.sunk | while | flops 275910400 | bytes 9257383 | solution.py:66
  336.7 4.4 conditional.6
  347.4 4.4 conditional.6
  358.1 4.4 conditional.6
  368.8 4.4 conditional.6
  379.6 4.4 conditional.6
  390.3 4.4 conditional.6
  401.0 4.4 conditional.6
  411.7 4.4 conditional.6
  422.4 4.4 conditional.6
  471.9 35.4 %psum.7 = f32[512]{0:T(512)S(1)} all-reduce(f32[512]{0:T(512)S(1)} %multiply_reduce_fusion), channel_id=1, replica_groups=mesh['ctx'=16,'tp'=16] {'tp'}, use_global_device_ids=true, to_apply=%region_19.20 | all-reduce | flops 512 | bytes 4096 | tf_op jit(solution)/shard_map/psum | solution.py:123
  (374 shorter events, 158.3 us)
Async XLA Ops:
  6.5 26.1 %copy-start = (s32[512]{0:T(512)S(1)}, s32[512]{0:T(512)}, u32[]{:S(2)}) copy-start(s32[512]{0:T(512)} %param.16) | copy-start | bytes 6148
  6.5 82.1 %all-gather.4.cloned.1.call-start = ((), (), s32[]{:S(2)}) async-start(), calls=%async_computation | async-start | bytes 8912896 | tf_op jit(solution)/shard_map/all_gather | solution.py:98
  7.3 160.1 %all-gather.6.cloned.1.call-start = ((), (), s32[]{:S(2)}) async-start(), calls=%async_computation.1 | async-start | bytes 8912896 | tf_op jit(solution)/shard_map/all_gather | solution.py:99
  471.3 36.0 %copy-start.1 = (f32[512]{0:T(512)S(1)}, f32[512]{0:T(512)}, u32[]{:S(2)}) copy-start(f32[512]{0:T(512)} %param.17) | copy-start | bytes 6148
Sparse Core Ops, SparseCore 0:
  10.1 78.5 all-gather.3
  91.4 75.8 all-gather.5
where the time goes:
time: 522 us; the launch traced here: 515 us
  loops' own time  122 us (23%)
  waiting for transfers between devices  114 us (22%)
  local copies, waits for them, and re-layouts  105 us (20%)
  matrix products  63.7 us (12%)
  blocking collectives  57.7 us (11%)
  other arithmetic  38.8 us (7%)
  between operations  13.5 us (3%)
    another operation x2, loops' own time, absorb(): lax.scan(visit, carry_state, (key_tiles, value_tiles, doc_tiles, tile_sta...  121 us
    all_gather x1, waiting for transfers between devices, local(): value_piece = lax.all_gather(values, 'ctx', axis=0, tiled=True)  57 us
    all_gather x1, waiting for transfers between devices, local(): key_piece = lax.all_gather(keys, 'ctx', axis=0, tiled=True)  55.3 us
    dot_general x18, matrix products, attend(): jnp.einsum('hrs,shd->rhd', weights.astype(jnp.bfloat16), value_tile, pref...  36.2 us
    psum x1, blocking collectives, local(): attn_sq = lax.psum(jnp.sum(attention * attention, axis=1), 'tp')  35.4 us
    dot_general x18, matrix products, attend(): jnp.einsum('rhd,shd->hrs', query_rows, key_tile, preferred_element_type=j...  27.5 us
    all_gather x1, blocking collectives, local(): doc_piece = lax.all_gather(doc_ids, 'ctx', axis=0, tiled=True)  22.3 us
    add x32, other arithmetic, visit(): key_pos = tile_start + jnp.arange(block_rows, dtype=jnp.int32)  22.1 us
  transfers between devices with their start and end apart: 2, of which 2 were waited for; matrix products, arithmetic and copies ran while one was open for 5% of the time, Pallas kernels for 0%

commit v1 on v0

v1 whole, which is shorter than its diff:
```python
import functools
import math

import jax
import jax.numpy as jnp
from jax import lax
from jax.experimental import pallas as pl
from jax.experimental.pallas import tpu as pltpu
from jax.sharding import PartitionSpec as P

D = 8192
HEAD_DIM = 128
CHUNK = 512
EPSILON = 1e-06
MASKED = -1e30
LOWEST = -1e20
LOG2_E = 1.4426950408889634
MESH = pl.DeviceIdType.MESH


def place():
    ctx = lax.axis_index("ctx")
    return ctx // 8, (ctx // 2) % 4, ctx % 2, lax.axis_index("tp")


def head_columns(head):
    return pl.ds(pl.multiple_of(head * HEAD_DIM, HEAD_DIM), HEAD_DIM)


def spread_kernel(q_ref, k_ref, v_ref, doc_ref, qo, ko, vo, do, q_send, q_recv, kv_send, kv_recv, fwd_send, cross_send, doc_send, doc_recv, own_sem):
    half, y, core, tp = place()
    mine = half * 8 + y * 2 + core

    barrier = pltpu.get_barrier_semaphore()
    for d in range(1, 16):
        pl.semaphore_signal(barrier, inc=1, device_id=((half * 8 + y * 2 + core + d) % 16, tp), device_id_type=MESH)
    pl.semaphore_wait(barrier, 15)

    kv = ((k_ref, ko), (v_ref, vo))

    def at(h, yy, c):
        return (h * 8 + yy * 2 + c, tp)

    started = []
    for a, (src, dst) in enumerate(kv):
        @pl.when(half == 0)
        def _():
            pltpu.make_async_remote_copy(
                src_ref=src.at[:, head_columns(y)], dst_ref=dst.at[mine], send_sem=cross_send.at[a, 0], recv_sem=kv_recv.at[a, mine],
                device_id=at(1, y, core), device_id_type=MESH).start()
    for d in (1, 3, 2):
        other = (y + d) % 4
        for a, (src, dst) in enumerate(kv):
            c = pltpu.make_async_remote_copy(
                src_ref=src.at[:, head_columns(other)], dst_ref=dst.at[mine], send_sem=kv_send.at[a, d], recv_sem=kv_recv.at[a, mine],
                device_id=at(half, other, core), device_id_type=MESH)
            c.start()
            started.append(c)
    for a, (src, dst) in enumerate(kv):
        c = pltpu.make_async_remote_copy(
            src_ref=src.at[:, head_columns(y)], dst_ref=dst.at[mine], send_sem=fwd_send.at[a, 0], recv_sem=kv_recv.at[a, mine],
            device_id=at(half, y, 1 - core), device_id_type=MESH)
        c.start()
        started.append(c)
    for d in range(1, 16):
        c = pltpu.make_async_remote_copy(
            src_ref=doc_ref, dst_ref=do.at[mine], send_sem=doc_send.at[d], recv_sem=doc_recv.at[16 - d],
            device_id=((mine + d) % 16, tp), device_id_type=MESH)
        c.start()
        started.append(c)
    for d in (1, 3, 2):
        other = (y + d) % 4
        c = pltpu.make_async_remote_copy(
            src_ref=q_ref.at[:, head_columns(other)], dst_ref=qo.at[y], send_sem=q_send.at[d], recv_sem=q_recv.at[4 - d],
            device_id=at(half, other, core), device_id_type=MESH)
        c.start()
        started.append(c)
    locals_ = [
        pltpu.make_async_copy(q_ref.at[:, head_columns(y)], qo.at[y], own_sem.at[0]),
        pltpu.make_async_copy(k_ref.at[:, head_columns(y)], ko.at[mine], own_sem.at[1]),
        pltpu.make_async_copy(v_ref.at[:, head_columns(y)], vo.at[mine], own_sem.at[2]),
        pltpu.make_async_copy(doc_ref, do.at[mine], own_sem.at[3]),
    ]
    for c in locals_:
        c.start()

    def landed(a, slot):
        dst = kv[a][1]
        pltpu.make_async_remote_copy(
            src_ref=dst.at[slot], dst_ref=dst.at[slot], send_sem=kv_send.at[a, 0], recv_sem=kv_recv.at[a, slot],
            device_id=at(half, y, 1 - core), device_id_type=MESH).wait_recv()

    for n, d in enumerate((1, 3, 2)):
        slot = half * 8 + ((y + d) % 4) * 2 + core
        for a in range(2):
            dst = kv[a][1]
            landed(a, slot)

            @pl.when(half == 0)
            def _():
                pltpu.make_async_remote_copy(
                    src_ref=dst.at[slot], dst_ref=dst.at[slot], send_sem=cross_send.at[a, n + 1], recv_sem=kv_recv.at[a, slot],
                    device_id=at(1, y, core), device_id_type=MESH).start()
            c = pltpu.make_async_remote_copy(
                src_ref=dst.at[slot], dst_ref=dst.at[slot], send_sem=fwd_send.at[a, n + 1], recv_sem=kv_recv.at[a, slot],
                device_id=at(half, y, 1 - core), device_id_type=MESH)
            c.start()
            started.append(c)

    order = (0, 1, 3, 2)
    @pl.when(half == 1)
    def _():
        for n, d in enumerate(order):
            slot = ((y + d) % 4) * 2 + core
            for a in range(2):
                dst = kv[a][1]
                landed(a, slot)
                pltpu.make_async_remote_copy(
                    src_ref=dst.at[slot], dst_ref=dst.at[slot], send_sem=cross_send.at[a, n], recv_sem=kv_recv.at[a, slot],
                    device_id=at(1, y, 1 - core), device_id_type=MESH).start()
        for n, d in enumerate(order):
            for a in range(2):
                landed(a, ((y + d) % 4) * 2 + 1 - core)

    for d in range(4):
        for a in range(2):
            landed(a, half * 8 + ((y + d) % 4) * 2 + 1 - core)
    for n in range(4):
        for a in range(2):
            dst = kv[a][1]
            pltpu.make_async_remote_copy(
                src_ref=dst.at[mine], dst_ref=dst.at[mine], send_sem=cross_send.at[a, n], recv_sem=kv_recv.at[a, mine],
                device_id=at(half, y, 1 - core), device_id_type=MESH).wait_send()
    for d in (1, 2, 3):
        pltpu.make_async_remote_copy(
            src_ref=qo.at[y], dst_ref=qo.at[y], send_sem=q_send.at[d], recv_sem=q_recv.at[d],
            device_id=at(half, y, 1 - core), device_id_type=MESH).wait_recv()
    for d in range(1, 16):
        pltpu.make_async_remote_copy(
            src_ref=doc_ref, dst_ref=do.at[mine], send_sem=doc_send.at[d], recv_sem=doc_recv.at[d],
            device_id=at(half, y, 1 - core), device_id_type=MESH).wait_recv()
    for c in started:
        c.wait_send()
    for c in locals_:
        c.wait()


def spread(queries, keys, values, docs):
    hbm = pl.BlockSpec(memory_space=pltpu.HBM)
    return pl.pallas_call(
        spread_kernel,
        name="spread",
        out_shape=[
            jax.ShapeDtypeStruct((4, CHUNK, HEAD_DIM), jnp.bfloat16),
            jax.ShapeDtypeStruct((16, CHUNK, HEAD_DIM), jnp.bfloat16),
            jax.ShapeDtypeStruct((16, CHUNK, HEAD_DIM), jnp.bfloat16),
            jax.ShapeDtypeStruct((16, 4, 128), jnp.int32),
        ],
        in_specs=[hbm] * 4,
        out_specs=[hbm] * 4,
        scratch_shapes=[
            pltpu.SemaphoreType.DMA((4,)),
            pltpu.SemaphoreType.DMA((4,)),
            pltpu.SemaphoreType.DMA((2, 4)),
            pltpu.SemaphoreType.DMA((2, 16)),
            pltpu.SemaphoreType.DMA((2, 4)),
            pltpu.SemaphoreType.DMA((2, 4)),
            pltpu.SemaphoreType.DMA((16,)),
            pltpu.SemaphoreType.DMA((16,)),
            pltpu.SemaphoreType.DMA((4,)),
        ],
        compiler_params=pltpu.CompilerParams(collective_id=0, has_side_effects=True),
    )(queries, keys, values, docs)


def attend_kernel(q_ref, k_ref, v_ref, doc_ref, o_ref):
    half, y, core, tp = place()
    scale = LOG2_E / math.sqrt(HEAD_DIM)
    seen = lax.broadcasted_iota(jnp.int32, (16, 4, 128), 0) < half * 8 + 8
    docs = doc_ref[...]
    first = jnp.sum(jnp.where(seen & (docs < 1), 1, 0))
    second = jnp.sum(jnp.where(seen & (docs < 2), 1, 0))

    def start_of(t):
        return jnp.where(t >= second, second, jnp.where(t >= first, first, 0))

    for n in range(4):
        chunk = half * 8 + n * 2 + core
        t0 = chunk * CHUNK
        q = q_ref[n]
        low = start_of(t0)
        high = start_of(t0 + CHUNK - 1)
        low_block = low // CHUNK
        whole = jnp.maximum(jnp.minimum((high + CHUNK - 1) // CHUNK, chunk), low_block)

        def block(k, state, masked):
            top, total, acc = state
            s = lax.dot_general(q, k_ref[k], (((1,), (1,)), ((), ())), preferred_element_type=jnp.float32) * scale
            if masked:
                rows = t0 + lax.broadcasted_iota(jnp.int32, (CHUNK, 1), 0)
                begin = start_of(rows)
                cols = k * CHUNK + lax.broadcasted_iota(jnp.int32, (CHUNK, CHUNK), 1)
                s = jnp.where((cols <= rows) & (cols >= begin), s, MASKED)
            new_top = jnp.maximum(top, jnp.max(s, axis=1, keepdims=True))
            p = jnp.exp2(s - new_top)
            factor = jnp.exp2(top - new_top)
            part = p[:, :128]
            for g in range(1, CHUNK // 128):
                part = part + p[:, g * 128:(g + 1) * 128]
            total = total * factor + part
            acc = acc * factor + jnp.dot(p.astype(jnp.bfloat16), v_ref[k], preferred_element_type=jnp.float32)
            return new_top, total, acc

        state = (jnp.full((CHUNK, 1), LOWEST, jnp.float32), jnp.zeros((CHUNK, 128), jnp.float32), jnp.zeros((CHUNK, HEAD_DIM), jnp.float32))
        state = lax.fori_loop(low_block, whole, lambda k, s: block(k, s, True), state)
        state = lax.fori_loop(whole, chunk, lambda k, s: block(k, s, False), state)
        top, total, acc = block(chunk, state, True)
        o_ref[n] = (acc / jnp.sum(total, axis=1, keepdims=True)).astype(jnp.bfloat16)


def attend(q, k, v, docs):
    return pl.pallas_call(
        attend_kernel,
        name="attend",
        out_shape=jax.ShapeDtypeStruct((4, CHUNK, HEAD_DIM), jnp.bfloat16),
        in_specs=[pl.BlockSpec(memory_space=pltpu.VMEM)] * 4,
        out_specs=pl.BlockSpec(memory_space=pltpu.VMEM),
        compiler_params=pltpu.CompilerParams(vmem_limit_bytes=48 * 1024 * 1024),
        cost_estimate=pl.CostEstimate(flops=3 * 10**9, bytes_accessed=5 * 2**20, transcendentals=6 * 10**6),
    )(q, k, v, docs)


def collect_kernel(o_ref, rows_ref, sums_ref, square, squares, o_send, o_recv, s_send, s_recv, own_sem):
    half, y, core, tp = place()

    barrier = pltpu.get_barrier_semaphore()
    for d in range(1, 4):
        pl.semaphore_signal(barrier, inc=1, device_id=(half * 8 + ((y + d) % 4) * 2 + core, tp), device_id_type=MESH)
    for d in range(1, 16):
        pl.semaphore_signal(barrier, inc=1, device_id=(half * 8 + y * 2 + core, (tp + d) % 16), device_id_type=MESH)
    pl.semaphore_wait(barrier, 18)

    sends = []
    for d in (2, 1, 3):
        other = (y + d) % 4
        c = pltpu.make_async_remote_copy(
            src_ref=o_ref.at[other], dst_ref=rows_ref.at[:, head_columns(y)], send_sem=o_send.at[d], recv_sem=o_recv.at[4 - d],
            device_id=(half * 8 + other * 2 + core, tp), device_id_type=MESH)
        c.start()
        sends.append(c)
    own = pltpu.make_async_copy(o_ref.at[y], rows_ref.at[:, head_columns(y)], own_sem.at[0])
    own.start()

    def add(head, sums):
        x = rows_ref[:, head_columns(head)].astype(jnp.float32)
        return sums + lax.dot_general(
            jnp.ones((8, HEAD_DIM), jnp.float32), x * x, (((1,), (1,)), ((), ())),
            precision=lax.Precision.HIGHEST, preferred_element_type=jnp.float32)

    own.wait()
    sums = add(y, jnp.zeros((8, CHUNK), jnp.float32))
    for d in (1, 3, 2):
        pltpu.make_async_remote_copy(
            src_ref=o_ref.at[y], dst_ref=rows_ref.at[:, head_columns((y + d) % 4)], send_sem=o_send.at[d], recv_sem=o_recv.at[d],
            device_id=(half * 8 + y * 2 + core, tp), device_id_type=MESH).wait_recv()
        sums = add((y + d) % 4, sums)
    square[...] = sums[:1]
    for d in range(1, 16):
        c = pltpu.make_async_remote_copy(
            src_ref=square, dst_ref=squares.at[tp], send_sem=s_send.at[d], recv_sem=s_recv.at[16 - d],
            device_id=(half * 8 + y * 2 + core, (tp + d) % 16), device_id_type=MESH)
        c.start()
        sends.append(c)
    total = square[...]
    for d in range(1, 16):
        pltpu.make_async_remote_copy(
            src_ref=square, dst_ref=squares.at[(tp + d) % 16], send_sem=s_send.at[d], recv_sem=s_recv.at[d],
            device_id=(half * 8 + y * 2 + core, tp), device_id_type=MESH).wait_recv()
    for d in range(1, 16):
        total = total + squares[(tp + d) % 16]
    sums_ref[...] = lax.rsqrt(total * (1.0 / D) + EPSILON)
    for c in sends:
        c.wait_send()


def collect(o):
    return pl.pallas_call(
        collect_kernel,
        name="collect",
        out_shape=[
            jax.ShapeDtypeStruct((CHUNK, 4 * HEAD_DIM), jnp.bfloat16),
            jax.ShapeDtypeStruct((1, CHUNK), jnp.float32),
        ],
        in_specs=[pl.BlockSpec(memory_space=pltpu.VMEM)],
        out_specs=[pl.BlockSpec(memory_space=pltpu.VMEM)] * 2,
        scratch_shapes=[
            pltpu.VMEM((1, CHUNK), jnp.float32),
            pltpu.VMEM((16, 1, CHUNK), jnp.float32),
            pltpu.SemaphoreType.DMA((4,)),
            pltpu.SemaphoreType.DMA((4,)),
            pltpu.SemaphoreType.DMA((16,)),
            pltpu.SemaphoreType.DMA((16,)),
            pltpu.SemaphoreType.DMA((1,)),
        ],
        compiler_params=pltpu.CompilerParams(collective_id=1, has_side_effects=True),
    )(o)


def local(queries, keys, values, doc_ids, attn_gain):
    q, k, v, docs = spread(queries, keys, values, doc_ids.reshape(4, 128))
    o = attend(q, k, v, docs)
    rows, factor = collect(o)
    blended = attn_gain[None, :] * rows.astype(jnp.float32) * factor.reshape(CHUNK, 1)
    return blended.astype(jnp.bfloat16)


def solution(mesh):
    placed = (P("ctx", "tp"), P("ctx", "tp"), P("ctx", "tp"), P("ctx"), P("tp"))
    return jax.shard_map(
        local, mesh=mesh, in_specs=placed, out_specs=P("ctx", "tp"), check_vma=False
    )
```

time: 522 us -> 84.4 us (0.16)
  the two profiles are of different devices: /device:TPU:4 before, /device:TPU:7 now
where the time goes in v1:
time: 84.4 us; the launch traced here: 84.1 us
  Pallas kernels  76.3 us (90%)
  local copies, waits for them, and re-layouts  5.76 us (7%)
  other arithmetic  1.98 us (2%)
    pallas_call x1, Pallas kernels, spread(): pl.pallas_call(spread_kernel, name='spread', out_shape=[jax.ShapeDtypeStr...  33.2 us
    pallas_call x1, Pallas kernels, attend(): pl.pallas_call(attend_kernel, name='attend', out_shape=jax.ShapeDtypeStru...  24.8 us
    pallas_call x1, Pallas kernels, collect(): pl.pallas_call(collect_kernel, name='collect', out_shape=[jax.ShapeDtypeS...  18.3 us
    unnamed x12, local copies, waits for them, and re-layouts  5.76 us
    convert_element_type x1, other arithmetic, local(): return blended.astype(jnp.bfloat16)  1.98 us

profile of v1, /device:TPU:7, one launch (start us, length us, event | category | flops | bytes accessed | tf_op | source)
XLA Modules:
  0.0 84.1 jit_solution(1197685074513227236)
XLA Ops:
  0.0 33.2 %spread.1 = (bf16[4,512,128]{2,1,0:T(8,128)(2,1)}, bf16[16,512,128]{2,1,0:T(8,128)(2,1)}, bf16[16,512,128]{2,1,0:T(8,128)(2,1)}, s32[16,4,128]{2,1,0:T(4,128)}) custom-call(bf16[512,512]{1,0:T(8,128)(2,1)} %q_ref.1, bf16[512,512]{1,0:T(8,128)(2,1)} %k_ref.1, bf16[512,512]{1,0:T(8,128)(2,1)} %v_ref.1, s32[4,128]{1,0:T(4,128)} %bitcast.2), custom_call_target="tpu_custom_call" | custom-call | tf_op jit(solution)/shard_map/spread/pallas_call | solution.py:150
  33.2 0.0 copy-start.1
  33.2 1.6 %copy-done.1 = bf16[16,512,128]{2,1,0:T(8,128)(2,1)S(1)} copy-done((bf16[16,512,128]{2,1,0:T(8,128)(2,1)S(1)}, bf16[16,512,128]{2,1,0:T(8,128)(2,1)}, u32[]{:S(2)}) %copy-start.1) | copy-done | bytes 2097176
  34.8 0.0 copy-start.2
  34.8 1.6 %copy-done.2 = bf16[16,512,128]{2,1,0:T(8,128)(2,1)S(1)} copy-done((bf16[16,512,128]{2,1,0:T(8,128)(2,1)S(1)}, bf16[16,512,128]{2,1,0:T(8,128)(2,1)}, u32[]{:S(2)}) %copy-start.2) | copy-done | bytes 2097176
  36.3 0.0 copy-start.3
  36.3 1.0 %copy-done.3 = bf16[4,512,128]{2,1,0:T(8,128)(2,1)S(1)} copy-done((bf16[4,512,128]{2,1,0:T(8,128)(2,1)S(1)}, bf16[4,512,128]{2,1,0:T(8,128)(2,1)}, u32[]{:S(2)}) %copy-start.3) | copy-done | bytes 524312
  37.4 0.0 copy-start.4
  37.4 0.8 copy-done.4
  38.1 0.0 copy-start.5
  38.1 24.8 %attend.1.o_ref = bf16[4,512,128]{2,1,0:T(8,128)(2,1)S(1)} custom-call(bf16[4,512,128]{2,1,0:T(8,128)(2,1)S(1)} %copy-done.3, bf16[16,512,128]{2,1,0:T(8,128)(2,1)S(1)} %copy-done.1, bf16[16,512,128]{2,1,0:T(8,128)(2,1)S(1)} %copy-done.2, s32[16,4,128]{2,1,0:T(4,128)S(1)} %copy-done.4), custom_call_target="tpu_custom_call" | custom-call | flops 3000000000 | bytes 5242880 | tf_op jit(solution)/shard_map/attend/pallas_call | solution.py:222
  63.0 0.0 copy-start
  63.0 0.8 copy-done
  63.8 18.3 %collect.1 = (bf16[512,512]{1,0:T(8,128)(2,1)}, f32[1,512]{1,0:T(1,128)}) custom-call(bf16[4,512,128]{2,1,0:T(8,128)(2,1)} %copy-done), custom_call_target="tpu_custom_call" | custom-call | tf_op jit(solution)/shard_map/collect/pallas_call | solution.py:287
  82.1 0.0 copy-done.5
  82.1 2.0 %multiply_convert_fusion = bf16[512,512]{1,0:T(8,128)(2,1)} fusion(bf16[512,512]{1,0:T(8,128)(2,1)} %get-tuple-element.15, f32[512]{0:T(512)} %bitcast.3, f32[512]{0:T(512)S(1)} %copy-done.5), kind=kLoop, calls=%fused_computation | loop fusion | flops 1048576 | bytes 1052672 | tf_op jit(solution)/shard_map/convert_element_type | solution.py:314
Async XLA Ops:
  33.2 1.6 %copy-start.1 = (bf16[16,512,128]{2,1,0:T(8,128)(2,1)S(1)}, bf16[16,512,128]{2,1,0:T(8,128)(2,1)}, u32[]{:S(2)}) copy-start(bf16[16,512,128]{2,1,0:T(8,128)(2,1)} %get-tuple-element.12.k_ref) | copy-start | bytes 6291460
  34.8 1.6 %copy-start.2 = (bf16[16,512,128]{2,1,0:T(8,128)(2,1)S(1)}, bf16[16,512,128]{2,1,0:T(8,128)(2,1)}, u32[]{:S(2)}) copy-start(bf16[16,512,128]{2,1,0:T(8,128)(2,1)} %get-tuple-element.13.v_ref) | copy-start | bytes 6291460
  36.3 1.0 %copy-start.3 = (bf16[4,512,128]{2,1,0:T(8,128)(2,1)S(1)}, bf16[4,512,128]{2,1,0:T(8,128)(2,1)}, u32[]{:S(2)}) copy-start(bf16[4,512,128]{2,1,0:T(8,128)(2,1)} %get-tuple-element.11.q_ref) | copy-start | bytes 1572868
  37.4 0.8 copy-start.4
  38.1 44.0 %copy-start.5 = (f32[512]{0:T(512)S(1)}, f32[512]{0:T(512)}, u32[]{:S(2)}) copy-start(f32[512]{0:T(512)} %param.9) | copy-start | bytes 6148
  63.0 0.8 copy-start

commit v2 on v0

v2 whole, which is shorter than its diff:
```python
import math

import jax
import jax.numpy as jnp
from jax import lax
from jax.experimental import pallas as pl
from jax.experimental.pallas import tpu as pltpu
from jax.sharding import PartitionSpec as P

D = 8192
HEAD_DIM = 128
CHUNK = 512
REACH = 5
EPSILON = 1e-06
MASKED = -1e29
LOWEST = -1e20
OTHER_DOC = -(2.0**100)
SCALE = 1.4426950408889634 / math.sqrt(HEAD_DIM)
ROWS = HEAD_DIM + 16
MESH = pl.DeviceIdType.MESH


def head_columns(head):
    return pl.ds(pl.multiple_of(head * HEAD_DIM, HEAD_DIM), HEAD_DIM)


def fused_kernel(
    q_ref, k_ref, v_ref, doc_ref, rows_ref, factor_ref,
    qbuf, kbuf, vbuf, docs, qfeat, kfeat, vt, sbuf, acc, top, obuf, part, parts, square, squares,
    q_send, q_recv, kv_send, kv_recv, fwd_send, cross_send, doc_send, doc_recv, own_sem,
    o_send, o_recv, p_send, p_recv, s_send, s_recv,
):
    ctx, tp = lax.axis_index("ctx"), lax.axis_index("tp")
    half, y, core = ctx // 8, (ctx // 2) % 4, ctx % 2
    mine = half * 8 + y * 2 + core

    def at(h, yy, c):
        return (h * 8 + yy * 2 + c, tp)

    sibling = at(half, y, 1 - core)

    barrier = pltpu.get_barrier_semaphore()
    for d in range(1, 16):
        pl.semaphore_signal(barrier, inc=1, device_id=((mine + d) % 16, tp), device_id_type=MESH)
    for d in range(1, 16):
        pl.semaphore_signal(barrier, inc=1, device_id=(mine, (tp + d) % 16), device_id_type=MESH)
    pl.semaphore_wait(barrier, 30)

    kv = ((k_ref, kbuf), (v_ref, vbuf))

    def remote(src, dst, send, recv, device):
        return pltpu.make_async_remote_copy(src_ref=src, dst_ref=dst, send_sem=send, recv_sem=recv, device_id=device, device_id_type=MESH)

    def doc_copy(d):
        return remote(doc_ref, docs.at[mine], doc_send.at[d], doc_recv.at[16 - d], ((mine + d) % 16, tp))

    def q_copy(d):
        other = (y + d) % 4
        return remote(q_ref.at[:, head_columns(other)], qbuf.at[y], q_send.at[d], q_recv.at[4 - d], at(half, other, core))

    def kv_copy(a, d):
        other = (y + d) % 4
        return remote(kv[a][0].at[:, head_columns(other)], kv[a][1].at[mine], kv_send.at[a, d], kv_recv.at[a, mine], at(half, other, core))

    def own_copy(a, send, device):
        return remote(kv[a][0].at[:, head_columns(y)], kv[a][1].at[mine], send, kv_recv.at[a, mine], device)

    def pass_on(a, slot, send, device):
        return remote(kv[a][1].at[slot], kv[a][1].at[slot], send, kv_recv.at[a, slot], device)

    def landed(slot):
        for a in range(2):
            pass_on(a, slot, kv_send.at[a, 0], sibling).wait_recv()

    for d in range(1, 16):
        doc_copy(d).start()
    locals_ = [
        pltpu.make_async_copy(doc_ref, docs.at[mine], own_sem.at[0]),
        pltpu.make_async_copy(q_ref.at[:, head_columns(y)], qbuf.at[y], own_sem.at[1]),
        pltpu.make_async_copy(k_ref.at[:, head_columns(y)], kbuf.at[mine], own_sem.at[2]),
        pltpu.make_async_copy(v_ref.at[:, head_columns(y)], vbuf.at[mine], own_sem.at[3]),
    ]
    for c in locals_:
        c.start()

    @pl.when(half == 0)
    def _():
        for a in range(2):
            own_copy(a, cross_send.at[a, 0], at(1, y, core)).start()
        for d in (1, 3, 2):
            for a in range(2):
                kv_copy(a, d).start()
        for d in (1, 3, 2):
            q_copy(d).start()

    @pl.when(half == 1)
    def _():
        for d in (1, 3, 2):
            q_copy(d).start()
        for d in (1, 3, 2):
            for a in range(2):
                kv_copy(a, d).start()

    for a in range(2):
        own_copy(a, fwd_send.at[a, 0], sibling).start()

    acc[...] = jnp.zeros(acc.shape, jnp.float32)
    top[...] = jnp.full(top.shape, LOWEST, jnp.float32)
    vt[:, HEAD_DIM:, :] = jnp.ones((2, ROWS - HEAD_DIM, CHUNK), jnp.bfloat16)

    for d in range(1, 16):
        remote(doc_ref, docs.at[mine], doc_send.at[d], doc_recv.at[d], sibling).wait_recv()
    for c in locals_:
        c.wait()

    def count(below):
        ones = jnp.where(docs[...] < below, 1.0, 0.0)
        return jnp.sum(jnp.sum(jnp.sum(ones, axis=0), axis=0, keepdims=True), axis=1, keepdims=True)

    second, third = count(1), count(2)
    lane = lax.broadcasted_iota(jnp.int32, (CHUNK, HEAD_DIM), 1)

    def doc_of(chunk):
        t = (chunk * CHUNK + lax.broadcasted_iota(jnp.int32, (CHUNK, HEAD_DIM), 0)).astype(jnp.float32)
        return jnp.where(t >= third, 2, jnp.where(t >= second, 1, 0))

    def key_features(s, _):
        kfeat[s] = jnp.where((lane < 3) & (lane != doc_of(s)), OTHER_DOC, 0.0).astype(jnp.bfloat16)
        return 0

    lax.fori_loop(0, half * 8 + 8, key_features, 0)

    def query_features(n, _):
        qfeat[n] = jnp.where(lane == doc_of(half * 8 + n * 2 + core), 1.0, 0.0).astype(jnp.bfloat16)
        return 0

    lax.fori_loop(0, 4, query_features, 0)

    @pl.when(half == 0)
    def _():
        for n, d in enumerate((1, 3, 2)):
            slot = ((y + d) % 4) * 2 + core
            landed(slot)
            for a in range(2):
                pass_on(a, slot, cross_send.at[a, n + 1], at(1, y, core)).start()
                pass_on(a, slot, fwd_send.at[a, n + 1], sibling).start()

    for d in (1, 3, 2):
        remote(qbuf.at[y], qbuf.at[y], q_send.at[d], q_recv.at[d], sibling).wait_recv()

    def score(slot, n):
        k = jnp.concatenate([kbuf[slot], kfeat[slot]], axis=1)
        q = jnp.concatenate([qbuf[n], qfeat[n]], axis=1)
        return lax.dot_general(k, q, (((1,), (1,)), ((), ())), preferred_element_type=jnp.float32) * SCALE

    def put_score(slot, n, buf):
        s = score(slot, n)
        sbuf[buf] = s
        return jnp.max(s, axis=0, keepdims=True)

    def absorb(state, s, s_top, buf):
        t, a = state
        new = jnp.maximum(t, s_top)
        p = jnp.exp2(s - new).astype(jnp.bfloat16)
        return new, a * jnp.exp2(t - new) + jnp.dot(vt[buf], p, preferred_element_type=jnp.float32)

    def visit(v, _):
        j, kind = v // (1 + half), v % (1 + half)
        d = j + j // 2 - 2 * (j // 3)
        pair = (y + d) % 4 + 4 * half * (1 - kind)
        slot_a, slot_b = pair * 2 + core, pair * 2 + 1 - core

        @pl.when((half == 1) & (v > 0))
        def _():
            landed(slot_a)
            for a in range(2):
                pass_on(a, slot_a, fwd_send.at[a, v], sibling).start()

        vt[0, :HEAD_DIM, :] = vbuf[slot_a].T
        landed(slot_b)
        vt[1, :HEAD_DIM, :] = vbuf[slot_b].T

        first = jnp.maximum(pair - 4 * half, 0)
        last = jnp.minimum(pair + REACH - 4 * half, 3)

        @pl.when(kind == 0)
        def _():
            s = score(slot_a, first)
            key = lax.broadcasted_iota(jnp.int32, (CHUNK, CHUNK), 0)
            query = lax.broadcasted_iota(jnp.int32, (CHUNK, CHUNK), 1)
            s = jnp.where(key <= query, s, MASKED)
            t, a = absorb((top[first], acc[first]), s, jnp.max(s, axis=0, keepdims=True), 0)
            top[first] = t
            acc[first] = a

            @pl.when(core == 1)
            def _():
                s = score(slot_b, first)
                t, a = absorb((top[first], acc[first]), s, jnp.max(s, axis=0, keepdims=True), 1)
                top[first] = t
                acc[first] = a

        begin = first + 1 - kind

        @pl.when(begin <= last)
        def _():
            def task(n, top_a):
                state = (top[n], acc[n])
                top_b = put_score(slot_b, n, 1)
                state = absorb(state, sbuf[0], top_a, 0)
                top_a = put_score(slot_a, jnp.minimum(n + 1, last), 0)
                t, a = absorb(state, sbuf[1], top_b, 1)
                top[n] = t
                acc[n] = a
                return top_a

            lax.fori_loop(begin, last + 1, task, put_score(slot_a, begin, 0))

        return 0

    lax.fori_loop(0, 4 + 4 * half, visit, 0)

    def o_copy(n):
        return remote(obuf.at[n], rows_ref.at[:, head_columns(y)], o_send.at[n], o_recv.at[y], at(half, n, core))

    def p_copy(n):
        return remote(part.at[n], parts.at[y], p_send.at[n], p_recv.at[y], at(half, n, core))

    def finish(n, _):
        a = acc[n]
        o = a[:HEAD_DIM] / a[HEAD_DIM:HEAD_DIM + 1]
        part[n] = jnp.sum(o * o, axis=0, keepdims=True)
        obuf[n] = o.T.astype(jnp.bfloat16)

        @pl.when(n != y)
        def _():
            p_copy(n).start()
            o_copy(n).start()
        return 0

    lax.fori_loop(0, 4, finish, 0)
    own = pltpu.make_async_copy(obuf.at[y], rows_ref.at[:, head_columns(y)], own_sem.at[4])
    own.start()
    total = part[y]
    for d in (1, 3, 2):
        other = (y + d) % 4
        remote(part.at[y], parts.at[other], p_send.at[y], p_recv.at[other], sibling).wait_recv()
        total = total + parts[other]
    square[...] = total

    def s_copy(d):
        return remote(square, squares.at[tp], s_send.at[d], s_recv.at[16 - d], (mine, (tp + d) % 16))

    for d in range(1, 16):
        s_copy(d).start()
    for d in range(1, 16):
        other = (tp + d) % 16
        remote(square, squares.at[other], s_send.at[d], s_recv.at[d], sibling).wait_recv()
        total = total + squares[other]
    factor_ref[...] = lax.rsqrt(total * (1.0 / D) + EPSILON)

    own.wait()
    for d in (1, 3, 2):
        other = (y + d) % 4
        remote(obuf.at[y], rows_ref.at[:, head_columns(other)], o_send.at[y], o_recv.at[other], sibling).wait_recv()
        o_copy(other).wait_send()
        p_copy(other).wait_send()
        q_copy(d).wait_send()
        for a in range(2):
            kv_copy(a, d).wait_send()
    for d in range(1, 16):
        s_copy(d).wait_send()
        doc_copy(d).wait_send()

    def sent(v, _):
        for a in range(2):
            pass_on(a, mine, fwd_send.at[a, v], sibling).wait_send()
        return 0

    lax.fori_loop(0, 4 + 4 * half, sent, 0)

    @pl.when(half == 0)
    def _():
        for n in range(4):
            for a in range(2):
                pass_on(a, mine, cross_send.at[a, n], sibling).wait_send()


def fused(queries, keys, values, docs):
    hbm = pl.BlockSpec(memory_space=pltpu.HBM)
    vmem = pl.BlockSpec(memory_space=pltpu.VMEM)
    dma = pltpu.SemaphoreType.DMA
    bf16, f32 = jnp.bfloat16, jnp.float32
    return pl.pallas_call(
        fused_kernel,
        name="fused",
        out_shape=[
            jax.ShapeDtypeStruct((CHUNK, 4 * HEAD_DIM), bf16),
            jax.ShapeDtypeStruct((1, CHUNK), f32),
        ],
        in_specs=[hbm] * 4,
        out_specs=[vmem] * 2,
        scratch_shapes=[
            pltpu.VMEM((4, CHUNK, HEAD_DIM), bf16),
            pltpu.VMEM((16, CHUNK, HEAD_DIM), bf16),
            pltpu.VMEM((16, CHUNK, HEAD_DIM), bf16),
            pltpu.VMEM((16, 4, 128), jnp.int32),
            pltpu.VMEM((4, CHUNK, HEAD_DIM), bf16),
            pltpu.VMEM((16, CHUNK, HEAD_DIM), bf16),
            pltpu.VMEM((2, ROWS, CHUNK), bf16),
            pltpu.VMEM((2, CHUNK, CHUNK), f32),
            pltpu.VMEM((4, ROWS, CHUNK), f32),
            pltpu.VMEM((4, 1, CHUNK), f32),
            pltpu.VMEM((4, CHUNK, HEAD_DIM), bf16),
            pltpu.VMEM((4, 1, CHUNK), f32),
            pltpu.VMEM((4, 1, CHUNK), f32),
            pltpu.VMEM((1, CHUNK), f32),
            pltpu.VMEM((16, 1, CHUNK), f32),
            dma((4,)), dma((4,)), dma((2, 4)), dma((2, 16)), dma((2, 8)), dma((2, 4)), dma((16,)), dma((16,)), dma((5,)),
            dma((4,)), dma((4,)), dma((4,)), dma((4,)), dma((16,)), dma((16,)),
        ],
        compiler_params=pltpu.CompilerParams(collective_id=0, has_side_effects=True, vmem_limit_bytes=40 * 2**20),
    )(queries, keys, values, docs)


def local(queries, keys, values, doc_ids, attn_gain):
    rows, factor = fused(queries, keys, values, doc_ids.reshape(4, 128))
    blended = attn_gain[None, :] * rows.astype(jnp.float32) * factor.reshape(CHUNK, 1)
    return blended.astype(jnp.bfloat16)


def solution(mesh):
    placed = (P("ctx", "tp"), P("ctx", "tp"), P("ctx", "tp"), P("ctx"), P("tp"))
    return jax.shard_map(
        local, mesh=mesh, in_specs=placed, out_specs=P("ctx", "tp"), check_vma=False
    )
```

time: 522 us -> 66.9 us (0.13)
  the two profiles are of different devices: /device:TPU:4 before, /device:TPU:20 now
where the time goes in v2:
time: 66.9 us; the launch traced here: 66.7 us
  Pallas kernels  61.2 us (91%)
  local copies, waits for them, and re-layouts  4.48 us (7%)
  other arithmetic  0.94 us (1%)
    pallas_call x1, Pallas kernels, fused(): pl.pallas_call(fused_kernel, name='fused', out_shape=[jax.ShapeDtypeStruc...  61.2 us
    unnamed x10, local copies, waits for them, and re-layouts  4.48 us

profile of v2, /device:TPU:20, one launch (start us, length us, event | category | flops | bytes accessed | tf_op | source)
XLA Modules:
  0.0 66.7 jit_solution(18366942626823573275)
XLA Ops:
  0.0 0.0 copy-start
  0.0 1.0 %copy-done = bf16[512,512]{1,0:T(8,128)(2,1)S(1)} copy-done((bf16[512,512]{1,0:T(8,128)(2,1)S(1)}, bf16[512,512]{1,0:T(8,128)(2,1)}, u32[]{:S(2)}) %copy-start) | copy-done | bytes 524312
  1.0 0.0 copy-start.1
  1.0 1.0 %copy-done.1 = bf16[512,512]{1,0:T(8,128)(2,1)S(1)} copy-done((bf16[512,512]{1,0:T(8,128)(2,1)S(1)}, bf16[512,512]{1,0:T(8,128)(2,1)}, u32[]{:S(2)}) %copy-start.1) | copy-done | bytes 524312
  2.1 0.0 copy-start.2
  2.1 1.0 %copy-done.2 = bf16[512,512]{1,0:T(8,128)(2,1)S(1)} copy-done((bf16[512,512]{1,0:T(8,128)(2,1)S(1)}, bf16[512,512]{1,0:T(8,128)(2,1)}, u32[]{:S(2)}) %copy-start.2) | copy-done | bytes 524312
  3.1 0.0 copy-start.3
  3.1 0.7 %copy-done.3 = s32[512]{0:T(512)S(1)} copy-done((s32[512]{0:T(512)S(1)}, s32[512]{0:T(512)}, u32[]{:S(2)}) %copy-start.3) | copy-done | bytes 2072
  3.8 61.2 %fused.1 = (bf16[512,512]{1,0:T(8,128)(2,1)S(1)}, f32[1,512]{1,0:T(1,128)S(1)}) custom-call(bf16[512,512]{1,0:T(8,128)(2,1)S(1)} %copy-done, bf16[512,512]{1,0:T(8,128)(2,1)S(1)} %copy-done.1, bf16[512,512]{1,0:T(8,128)(2,1)S(1)} %copy-done.2, s32[4,128]{1,0:T(4,128)S(1)} %bitcast.2), custom_call_target="tpu_custom_call" | custom-call | tf_op jit(solution)/shard_map/fused/pallas_call | solution.py:294
  65.0 0.0 copy-start.4
  65.0 0.7 %copy-done.4 = f32[512]{0:T(512)S(1)} copy-done((f32[512]{0:T(512)S(1)}, f32[512]{0:T(512)}, u32[]{:S(2)}) %copy-start.4) | copy-done | bytes 2072
  65.7 0.9 %multiply_convert_fusion = bf16[512,512]{1,0:T(8,128)(2,1)} fusion(bf16[512,512]{1,0:T(8,128)(2,1)S(1)} %get-tuple-element.7, f32[512]{0:T(512)S(1)} %bitcast.3, f32[512]{0:T(512)S(1)} %copy-done.4), kind=kLoop, calls=%fused_computation | loop fusion | flops 1048576 | bytes 1052672 | tf_op jit(solution)/shard_map/convert_element_type | solution.py:329
Async XLA Ops:
  0.0 1.0 %copy-start = (bf16[512,512]{1,0:T(8,128)(2,1)S(1)}, bf16[512,512]{1,0:T(8,128)(2,1)}, u32[]{:S(2)}) copy-start(bf16[512,512]{1,0:T(8,128)(2,1)} %q_ref.1) | copy-start | bytes 1572868
  1.0 1.0 %copy-start.1 = (bf16[512,512]{1,0:T(8,128)(2,1)S(1)}, bf16[512,512]{1,0:T(8,128)(2,1)}, u32[]{:S(2)}) copy-start(bf16[512,512]{1,0:T(8,128)(2,1)} %k_ref.1) | copy-start | bytes 1572868
  2.1 1.0 %copy-start.2 = (bf16[512,512]{1,0:T(8,128)(2,1)S(1)}, bf16[512,512]{1,0:T(8,128)(2,1)}, u32[]{:S(2)}) copy-start(bf16[512,512]{1,0:T(8,128)(2,1)} %v_ref.1) | copy-start | bytes 1572868
  3.1 0.7 %copy-start.3 = (s32[512]{0:T(512)S(1)}, s32[512]{0:T(512)}, u32[]{:S(2)}) copy-start(s32[512]{0:T(512)} %param.8) | copy-start | bytes 6148
  65.0 0.7 %copy-start.4 = (f32[512]{0:T(512)S(1)}, f32[512]{0:T(512)}, u32[]{:S(2)}) copy-start(f32[512]{0:T(512)} %param.9) | copy-start | bytes 6148

commit v3 on v2

--- a/solution.py
+++ b/solution.py
@@ -87,26 +87,26 @@
     def _():
         for a in range(2):
             own_copy(a, cross_send.at[a, 0], at(1, y, core)).start()
-        for d in (1, 3, 2):
+        for d in (1, 3):
             for a in range(2):
                 kv_copy(a, d).start()
+
+    @pl.when(half == 1)
+    def _():
         for d in (1, 3, 2):
             q_copy(d).start()
 
-    @pl.when(half == 1)
-    def _():
-        for d in (1, 3, 2):
-            q_copy(d).start()
-        for d in (1, 3, 2):
-            for a in range(2):
-                kv_copy(a, d).start()
-
     for a in range(2):
         own_copy(a, fwd_send.at[a, 0], sibling).start()
 
     acc[...] = jnp.zeros(acc.shape, jnp.float32)
     top[...] = jnp.full(top.shape, LOWEST, jnp.float32)
-    vt[:, HEAD_DIM:, :] = jnp.ones((2, ROWS - HEAD_DIM, CHUNK), jnp.bfloat16)
+
+    def ones_rows(n, _):
+        vt[n, HEAD_DIM:, :] = jnp.ones((ROWS - HEAD_DIM, CHUNK), jnp.bfloat16)
+        return 0
+
+    lax.fori_loop(0, 8 + 8 * half, ones_rows, 0)
 
     for d in range(1, 16):
         remote(doc_ref, docs.at[mine], doc_send.at[d], doc_recv.at[d], sibling).wait_recv()
@@ -136,17 +136,24 @@
 
     lax.fori_loop(0, 4, query_features, 0)
 
-    @pl.when(half == 0)
-    def _():
-        for n, d in enumerate((1, 3, 2)):
-            slot = ((y + d) % 4) * 2 + core
-            landed(slot)
-            for a in range(2):
-                pass_on(a, slot, cross_send.at[a, n + 1], at(1, y, core)).start()
-                pass_on(a, slot, fwd_send.at[a, n + 1], sibling).start()
-
-    for d in (1, 3, 2):
-        remote(qbuf.at[y], qbuf.at[y], q_send.at[d], q_recv.at[d], sibling).wait_recv()
+    def along(j):
+        return j + j // 2 - 2 * (j // 3)
+
+    falling = ((y + 1) // 2 + 1) % 2
+    swapped = (y // 2) * (1 - falling)
+
+    def across(j):
+        return falling * ((4 - j) % 4) + (1 - falling) * (j + swapped * (j // 2) * (5 - 2 * j))
+
+    def pass_to_sibling(slot, n):
+        for a in range(2):
+            pass_on(a, slot, fwd_send.at[a, n], sibling).start()
+
+    def turn(slot):
+        vt[slot, :HEAD_DIM, :] = vbuf[slot].T
+
+    def q_landed(d):
+        remote(qbuf.at[y], qbuf.at[y], q_send.at[0], q_recv.at[d], sibling).wait_recv()
 
     def score(slot, n):
         k = jnp.concatenate([kbuf[slot], kfeat[slot]], axis=1)
@@ -158,67 +165,48 @@
         sbuf[buf] = s
         return jnp.max(s, axis=0, keepdims=True)
 
-    def absorb(state, s, s_top, buf):
+    def absorb(state, s, s_top, slot):
         t, a = state
         new = jnp.maximum(t, s_top)
         p = jnp.exp2(s - new).astype(jnp.bfloat16)
-        return new, a * jnp.exp2(t - new) + jnp.dot(vt[buf], p, preferred_element_type=jnp.float32)
-
-    def visit(v, _):
-        j, kind = v // (1 + half), v % (1 + half)
-        d = j + j // 2 - 2 * (j // 3)
-        pair = (y + d) % 4 + 4 * half * (1 - kind)
-        slot_a, slot_b = pair * 2 + core, pair * 2 + 1 - core
-
-        @pl.when((half == 1) & (v > 0))
-        def _():
-            landed(slot_a)
-            for a in range(2):
-                pass_on(a, slot_a, fwd_send.at[a, v], sibling).start()
-
-        vt[0, :HEAD_DIM, :] = vbuf[slot_a].T
-        landed(slot_b)
-        vt[1, :HEAD_DIM, :] = vbuf[slot_b].T
-
-        first = jnp.maximum(pair - 4 * half, 0)
-        last = jnp.minimum(pair + REACH - 4 * half, 3)
-
-        @pl.when(kind == 0)
-        def _():
-            s = score(slot_a, first)
+        return new, a * jnp.exp2(t - new) + jnp.dot(vt[slot], p, preferred_element_type=jnp.float32)
+
+    def diagonal(slot_a, slot_b, n):
+        def masked():
             key = lax.broadcasted_iota(jnp.int32, (CHUNK, CHUNK), 0)
             query = lax.broadcasted_iota(jnp.int32, (CHUNK, CHUNK), 1)
-            s = jnp.where(key <= query, s, MASKED)
-            t, a = absorb((top[first], acc[first]), s, jnp.max(s, axis=0, keepdims=True), 0)
-            top[first] = t
-            acc[first] = a
-
-            @pl.when(core == 1)
-            def _():
-                s = score(slot_b, first)
-                t, a = absorb((top[first], acc[first]), s, jnp.max(s, axis=0, keepdims=True), 1)
-                top[first] = t
-                acc[first] = a
-
-        begin = first + 1 - kind
-
-        @pl.when(begin <= last)
+            return jnp.where(key <= query, score(slot_a, n), MASKED)
+
+        @pl.when(core == 0)
         def _():
-            def task(n, top_a):
-                state = (top[n], acc[n])
-                top_b = put_score(slot_b, n, 1)
-                state = absorb(state, sbuf[0], top_a, 0)
-                top_a = put_score(slot_a, jnp.minimum(n + 1, last), 0)
-                t, a = absorb(state, sbuf[1], top_b, 1)
-                top[n] = t
-                acc[n] = a
-                return top_a
-
-            lax.fori_loop(begin, last + 1, task, put_score(slot_a, begin, 0))
-
-        return 0
-
-    lax.fori_loop(0, 4 + 4 * half, visit, 0)
+            s = masked()
+            t, a = absorb((top[n], acc[n]), s, jnp.max(s, axis=0, keepdims=True), slot_a)
+            top[n] = t
+            acc[n] = a
+
+        @pl.when(core == 1)
+        def _():
+            s_b, s_a = score(slot_b, n), masked()
+            t = top[n]
+            new = jnp.maximum(t, jnp.maximum(jnp.max(s_a, axis=0, keepdims=True), jnp.max(s_b, axis=0, keepdims=True)))
+            p_b = jnp.exp2(s_b - new).astype(jnp.bfloat16)
+            p_a = jnp.exp2(s_a - new).astype(jnp.bfloat16)
+            top[n] = new
+            acc[n] = (
+                acc[n] * jnp.exp2(t - new)
+                + jnp.dot(vt[slot_b], p_b, preferred_element_type=jnp.float32)
+                + jnp.dot(vt[slot_a], p_a, preferred_element_type=jnp.float32)
+            )
+
+    def whole(slot_a, slot_b, n, next_a, next_n, top_a):
+        state = (top[n], acc[n])
+        top_b = put_score(slot_b, n, 1)
+        state = absorb(state, sbuf[0], top_a, slot_a)
+        top_a = put_score(next_a, next_n, 0)
+        t, a = absorb(state, sbuf[1], top_b, slot_b)
+        top[n] = t
+        acc[n] = a
+        return top_a
 
     def o_copy(n):
         return remote(obuf.at[n], rows_ref.at[:, head_columns(y)], o_send.at[n], o_recv.at[y], at(half, n, core))
@@ -238,7 +226,141 @@
             o_copy(n).start()
         return 0
 
-    lax.fori_loop(0, 4, finish, 0)
+    @pl.when(half == 0)
+    def _():
+        turn(mine)
+        for d in (1, 3):
+            for a in range(2):
+                kv_copy(a, d).wait_send()
+        for a in range(2):
+            kv_copy(a, 2).start()
+
+        def relay(j, _):
+            slot = ((y + across(j)) % 4) * 2 + core
+            landed(slot)
+
+            @pl.when(j == 3)
+            def _():
+                for a in range(2):
+                    kv_copy(a, 2).wait_send()
+                for d in (1, 3, 2):
+                    q_copy(d).start()
+
+            for a in range(2):
+                pass_on(a, slot, cross_send.at[a, j - 1], sibling).wait_send()
+                pass_on(a, slot, cross_send.at[a, j], at(1, y, core)).start()
+            pass_to_sibling(slot, j)
+            turn(slot)
+            return 0
+
+        lax.fori_loop(1, 4, relay, 0)
+
+        def from_sibling(j, _):
+            slot = ((y + across(j)) % 4) * 2 + 1 - core
+            landed(slot)
+            turn(slot)
+            return 0
+
+        lax.fori_loop(0, 4, from_sibling, 0)
+
+        def rows_of(j, _):
+            d = along(j)
+            n = (y + d) % 4
+
+            @pl.when(j > 0)
+            def _():
+                q_landed(d)
+
+            diagonal(n * 2 + core, n * 2 + 1 - core, n)
+
+            @pl.when(n > 0)
+            def _():
+                def step(p, top_a):
+                    return whole(p * 2 + core, p * 2 + 1 - core, n, jnp.minimum(p + 1, n - 1) * 2 + core, n, top_a)
+
+                lax.fori_loop(0, n, step, put_score(core, n, 0))
+
+            finish(n, 0)
+            return 0
+
+        lax.fori_loop(0, 4, rows_of, 0)
+
+    @pl.when(half == 1)
+    def _():
+        def visited(v):
+            j, kind = v // 2, v % 2
+            d = (1 - kind) * along(j) + kind * across(j)
+            return (y + d) % 4 + 4 * (1 - kind), kind
+
+        def forward(v, _):
+            slot = visited(v)[0] * 2 + core
+            landed(slot)
+            pass_to_sibling(slot, v)
+            turn(slot)
+            return 0
+
+        turn(mine)
+        for d in (1, 3, 2):
+            q_copy(d).wait_send()
+        for d in (1, 3):
+            for a in range(2):
+                kv_copy(a, d).start()
+        forward(1, 0)
+        for d in (1, 3, 2):
+            q_landed(d)
+
+        def visit(v, _):
+            pair, kind = visited(v)
+            slot_a, slot_b = pair * 2 + core, pair * 2 + 1 - core
+            first = (pair - 4) * (1 - kind)
+            count = kind * jnp.minimum(pair + 2, 4) + (1 - kind) * (3 - first)
+            begin = (first + 1) * (1 - kind)
+            final = v == 7
+
+            @pl.when(final)
+            def _():
+                lax.fori_loop(count, 4, finish, 0)
+
+            @pl.when(v == 2)
+            def _():
+                for d in (1, 3):
+                    for a in range(2):
+                        kv_copy(a, d).wait_send()
+                for a in range(2):
+                    kv_copy(a, 2).start()
+
+            for at_visit, low, high in ((2, 2, 5), (5, 5, 7), (7, 7, 8)):
+                @pl.when(v == at_visit)
+                def _():
+                    lax.fori_loop(low, high, forward, 0)
+
+            landed(slot_b)
+            turn(slot_b)
+
+            @pl.when(kind == 0)
+            def _():
+                diagonal(slot_a, slot_b, first)
+
+            @pl.when(count > 0)
+            def _():
+                def nth(i):
+                    return begin + (i + kind * (y + 1)) % count
+
+                def step(i, top_a):
+                    n = nth(i)
+                    top_a = whole(slot_a, slot_b, n, slot_a, nth(jnp.minimum(i + 1, count - 1)), top_a)
+
+                    @pl.when(final)
+                    def _():
+                        finish(n, 0)
+                    return top_a
+
+                lax.fori_loop(0, count, step, put_score(slot_a, nth(0), 0))
+
+            return 0
+
+        lax.fori_loop(0, 8, visit, 0)
+
     own = pltpu.make_async_copy(obuf.at[y], rows_ref.at[:, head_columns(y)], own_sem.at[4])
     own.start()
     total = part[y]
@@ -265,9 +387,10 @@
         remote(obuf.at[y], rows_ref.at[:, head_columns(other)], o_send.at[y], o_recv.at[other], sibling).wait_recv()
         o_copy(other).wait_send()
         p_copy(other).wait_send()
-        q_copy(d).wait_send()
-        for a in range(2):
-            kv_copy(a, d).wait_send()
+
+        @pl.when(half == 0)
+        def _():
+            q_copy(d).wait_send()
     for d in range(1, 16):
         s_copy(d).wait_send()
         doc_copy(d).wait_send()
@@ -281,9 +404,13 @@
 
     @pl.when(half == 0)
     def _():
-        for n in range(4):
-            for a in range(2):
-                pass_on(a, mine, cross_send.at[a, n], sibling).wait_send()
+        for a in range(2):
+            pass_on(a, mine, cross_send.at[a, 3], sibling).wait_send()
+
+    @pl.when(half == 1)
+    def _():
+        for a in range(2):
+            kv_copy(a, 2).wait_send()
 
 
 def fused(queries, keys, values, docs):
@@ -307,7 +434,7 @@
             pltpu.VMEM((16, 4, 128), jnp.int32),
             pltpu.VMEM((4, CHUNK, HEAD_DIM), bf16),
             pltpu.VMEM((16, CHUNK, HEAD_DIM), bf16),
-            pltpu.VMEM((2, ROWS, CHUNK), bf16),
+            pltpu.VMEM((16, ROWS, CHUNK), bf16),
             pltpu.VMEM((2, CHUNK, CHUNK), f32),
             pltpu.VMEM((4, ROWS, CHUNK), f32),
             pltpu.VMEM((4, 1, CHUNK), f32),
@@ -319,7 +446,7 @@
             dma((4,)), dma((4,)), dma((2, 4)), dma((2, 16)), dma((2, 8)), dma((2, 4)), dma((16,)), dma((16,)), dma((5,)),
             dma((4,)), dma((4,)), dma((4,)), dma((4,)), dma((16,)), dma((16,)),
         ],
-        compiler_params=pltpu.CompilerParams(collective_id=0, has_side_effects=True, vmem_limit_bytes=40 * 2**20),
+        compiler_params=pltpu.CompilerParams(collective_id=0, has_side_effects=True, vmem_limit_bytes=62 * 10**6),
     )(queries, keys, values, docs)
 
 

time: 66.9 us -> 58.2 us (0.87)
  the two profiles are of different devices: /device:TPU:20 before, /device:TPU:4 now
where the time goes in v3:
time: 58.2 us; the launch traced here: 58.1 us
  Pallas kernels  55.4 us (95%)
  other arithmetic  1.98 us (3%)
  local copies, waits for them, and re-layouts  0.68 us (1%)
    pallas_call x1, Pallas kernels, fused(): pl.pallas_call(fused_kernel, name='fused', out_shape=[jax.ShapeDtypeStruc...  55.4 us
    convert_element_type x1, other arithmetic, local(): return blended.astype(jnp.bfloat16)  1.98 us

profile of v3, /device:TPU:4, one launch (start us, length us, event | category | flops | bytes accessed | tf_op | source)
XLA Modules:
  0.0 58.1 jit_solution(17595341732066726590)
XLA Ops:
  0.0 55.4 %fused.1 = (bf16[512,512]{1,0:T(8,128)(2,1)}, f32[1,512]{1,0:T(1,128)}) custom-call(bf16[512,512]{1,0:T(8,128)(2,1)} %q_ref.1, bf16[512,512]{1,0:T(8,128)(2,1)} %k_ref.1, bf16[512,512]{1,0:T(8,128)(2,1)} %v_ref.1, s32[4,128]{1,0:T(4,128)} %bitcast.2), custom_call_target="tpu_custom_call" | custom-call | tf_op jit(solution)/shard_map/fused/pallas_call | solution.py:421
  55.4 0.0 copy-start.1
  55.4 0.0 copy-start
  55.5 0.6 %copy-done.1 = f32[1,512]{1,0:T(1,128)S(1)} copy-done((f32[1,512]{1,0:T(1,128)S(1)}, f32[1,512]{1,0:T(1,128)}, u32[]{:S(2)}) %copy-start.1) | copy-done | bytes 2072
  56.1 0.0 copy-done
  56.1 2.0 %multiply_convert_fusion = bf16[512,512]{1,0:T(8,128)(2,1)} fusion(bf16[512,512]{1,0:T(8,128)(2,1)} %get-tuple-element.7, f32[512]{0:T(512)S(1)} %bitcast.3, f32[512]{0:T(512)S(1)} %copy-done), kind=kLoop, calls=%fused_computation | loop fusion | flops 1048576 | bytes 1052672 | tf_op jit(solution)/shard_map/convert_element_type | solution.py:456
Async XLA Ops:
  55.4 0.7 %copy-start.1 = (f32[1,512]{1,0:T(1,128)S(1)}, f32[1,512]{1,0:T(1,128)}, u32[]{:S(2)}) copy-start(f32[1,512]{1,0:T(1,128)} %get-tuple-element.8) | copy-start | bytes 6148
  55.4 0.7 %copy-start = (f32[512]{0:T(512)S(1)}, f32[512]{0:T(512)}, u32[]{:S(2)}) copy-start(f32[512]{0:T(512)} %param.9) | copy-start | bytes 6148

commit v4 on v3

--- a/solution.py
+++ b/solution.py
@@ -216,13 +216,17 @@
 
     def finish(n, _):
         a = acc[n]
-        o = a[:HEAD_DIM] / a[HEAD_DIM:HEAD_DIM + 1]
+        o = a[:HEAD_DIM] * (1.0 / a[HEAD_DIM:HEAD_DIM + 1])
         part[n] = jnp.sum(o * o, axis=0, keepdims=True)
-        obuf[n] = o.T.astype(jnp.bfloat16)
 
         @pl.when(n != y)
         def _():
             p_copy(n).start()
+
+        obuf[n] = o.T.astype(jnp.bfloat16)
+
+        @pl.when(n != y)
+        def _():
             o_copy(n).start()
         return 0
 
@@ -288,7 +292,8 @@
     @pl.when(half == 1)
     def _():
         def visited(v):
-            j, kind = v // 2, v % 2
+            kind = jnp.where((v == 1) | (v == 4) | (v > 5), 1, 0)
+            j = jnp.where(v < 2, 0, jnp.where((v == 2) | (v == 4), 1, jnp.where((v == 3) | (v == 6), 2, 3)))
             d = (1 - kind) * along(j) + kind * across(j)
             return (y + d) % 4 + 4 * (1 - kind), kind
 
@@ -317,6 +322,12 @@
             begin = (first + 1) * (1 - kind)
             final = v == 7
 
+            def ahead():
+                for at_visit, low, high in ((1, 2, 4), (2, 4, 5), (4, 5, 6), (5, 6, 7), (6, 7, 8)):
+                    @pl.when(v == at_visit)
+                    def _():
+                        lax.fori_loop(low, high, forward, 0)
+
             @pl.when(final)
             def _():
                 lax.fori_loop(count, 4, finish, 0)
@@ -329,14 +340,11 @@
                 for a in range(2):
                     kv_copy(a, 2).start()
 
-            for at_visit, low, high in ((2, 2, 5), (5, 5, 7), (7, 7, 8)):
-                @pl.when(v == at_visit)
-                def _():
-                    lax.fori_loop(low, high, forward, 0)
-
             landed(slot_b)
             turn(slot_b)
 
+            pl.when(count == 0)(ahead)
+
             @pl.when(kind == 0)
             def _():
                 diagonal(slot_a, slot_b, first)
@@ -348,6 +356,7 @@
 
                 def step(i, top_a):
                     n = nth(i)
+                    pl.when(i == count - 1)(ahead)
                     top_a = whole(slot_a, slot_b, n, slot_a, nth(jnp.minimum(i + 1, count - 1)), top_a)
 
                     @pl.when(final)
@@ -446,7 +455,7 @@
             dma((4,)), dma((4,)), dma((2, 4)), dma((2, 16)), dma((2, 8)), dma((2, 4)), dma((16,)), dma((16,)), dma((5,)),
             dma((4,)), dma((4,)), dma((4,)), dma((4,)), dma((16,)), dma((16,)),
         ],
-        compiler_params=pltpu.CompilerParams(collective_id=0, has_side_effects=True, vmem_limit_bytes=62 * 10**6),
+        compiler_params=pltpu.CompilerParams(collective_id=0, has_side_effects=True, vmem_limit_bytes=56 * 10**6),
     )(queries, keys, values, docs)
 
 

time: 58.2 us -> 56.2 us (0.966)
  Pallas kernels: 55.4 us -> 53.7 us
  other arithmetic: 1.98 us -> 0.94 us
  local copies, waits for them, and re-layouts: 0.68 us -> 1.36 us
    pallas_call x1, Pallas kernels: 55.4 us -> 53.7 us  [fused(): pl.pallas_call(fused_kernel, name='fused', out_shape=[jax.ShapeDtypeStruc...]
    convert_element_type x1, other arithmetic: 1.98 us -> 0.94 us  [local(): return blended.astype(jnp.bfloat16)]
    unnamed x4, local copies, waits for them, and re-layouts: 0.68 us -> 1.36 us
where the time goes in v4:
time: 56.2 us; the launch traced here: 56.1 us
  Pallas kernels  53.7 us (96%)
  local copies, waits for them, and re-layouts  1.36 us (2%)
  other arithmetic  0.94 us (2%)
    pallas_call x1, Pallas kernels, fused(): pl.pallas_call(fused_kernel, name='fused', out_shape=[jax.ShapeDtypeStruc...  53.7 us
    unnamed x4, local copies, waits for them, and re-layouts  1.36 us

profile of v4, /device:TPU:4, one launch (start us, length us, event | category | flops | bytes accessed | tf_op | source)
XLA Modules:
  0.0 56.1 jit_solution(6468553724852868009)
XLA Ops:
  0.0 0.0 copy-start
  0.0 0.7 %copy-done = s32[512]{0:T(512)S(1)} copy-done((s32[512]{0:T(512)S(1)}, s32[512]{0:T(512)}, u32[]{:S(2)}) %copy-start) | copy-done | bytes 2072
  0.7 53.7 %fused.1 = (bf16[512,512]{1,0:T(8,128)(2,1)S(1)}, f32[1,512]{1,0:T(1,128)S(1)}) custom-call(bf16[512,512]{1,0:T(8,128)(2,1)} %q_ref.1, bf16[512,512]{1,0:T(8,128)(2,1)} %k_ref.1, bf16[512,512]{1,0:T(8,128)(2,1)} %v_ref.1, s32[4,128]{1,0:T(4,128)S(1)} %bitcast.2), custom_call_target="tpu_custom_call" | custom-call | tf_op jit(solution)/shard_map/fused/pallas_call | solution.py:430
  54.4 0.0 copy-start.1
  54.4 0.7 %copy-done.1 = f32[512]{0:T(512)S(1)} copy-done((f32[512]{0:T(512)S(1)}, f32[512]{0:T(512)}, u32[]{:S(2)}) %copy-start.1) | copy-done | bytes 2072
  55.1 0.9 %multiply_convert_fusion = bf16[512,512]{1,0:T(8,128)(2,1)} fusion(bf16[512,512]{1,0:T(8,128)(2,1)S(1)} %get-tuple-element.7, f32[512]{0:T(512)S(1)} %bitcast.3, f32[512]{0:T(512)S(1)} %copy-done.1), kind=kLoop, calls=%fused_computation | loop fusion | flops 1048576 | bytes 1052672 | tf_op jit(solution)/shard_map/convert_element_type | solution.py:465
Async XLA Ops:
  0.0 0.7 %copy-start = (s32[512]{0:T(512)S(1)}, s32[512]{0:T(512)}, u32[]{:S(2)}) copy-start(s32[512]{0:T(512)} %param.8) | copy-start | bytes 6148
  54.4 0.7 %copy-start.1 = (f32[512]{0:T(512)S(1)}, f32[512]{0:T(512)}, u32[]{:S(2)}) copy-start(f32[512]{0:T(512)} %param.9) | copy-start | bytes 6148

commit v5 on v4

--- a/solution.py
+++ b/solution.py
@@ -25,8 +25,8 @@
 
 
 def fused_kernel(
-    q_ref, k_ref, v_ref, doc_ref, rows_ref, factor_ref,
-    qbuf, kbuf, vbuf, docs, qfeat, kfeat, vt, sbuf, acc, top, obuf, part, parts, square, squares,
+    q_ref, k_ref, v_ref, doc_ref, gain_ref, rows_ref, factor_ref,
+    gain, qbuf, kbuf, vbuf, docs, qfeat, kfeat, vt, sbuf, acc, top, obuf, part, parts, square, squares,
     q_send, q_recv, kv_send, kv_recv, fwd_send, cross_send, doc_send, doc_recv, own_sem,
     o_send, o_recv, p_send, p_recv, s_send, s_recv,
 ):
@@ -77,6 +77,7 @@
     locals_ = [
         pltpu.make_async_copy(doc_ref, docs.at[mine], own_sem.at[0]),
         pltpu.make_async_copy(q_ref.at[:, head_columns(y)], qbuf.at[y], own_sem.at[1]),
+        pltpu.make_async_copy(gain_ref.at[:, head_columns(y)], gain, own_sem.at[5]),
         pltpu.make_async_copy(k_ref.at[:, head_columns(y)], kbuf.at[mine], own_sem.at[2]),
         pltpu.make_async_copy(v_ref.at[:, head_columns(y)], vbuf.at[mine], own_sem.at[3]),
     ]
@@ -86,18 +87,19 @@
     @pl.when(half == 0)
     def _():
         for a in range(2):
+            for d in (1, 3):
+                kv_copy(a, d).start()
             own_copy(a, cross_send.at[a, 0], at(1, y, core)).start()
-        for d in (1, 3):
-            for a in range(2):
-                kv_copy(a, d).start()
 
     @pl.when(half == 1)
     def _():
         for d in (1, 3, 2):
             q_copy(d).start()
 
-    for a in range(2):
-        own_copy(a, fwd_send.at[a, 0], sibling).start()
+    @pl.when(half == 1)
+    def _():
+        for a in range(2):
+            own_copy(a, fwd_send.at[a, 0], sibling).start()
 
     acc[...] = jnp.zeros(acc.shape, jnp.float32)
     top[...] = jnp.full(top.shape, LOWEST, jnp.float32)
@@ -223,7 +225,7 @@
         def _():
             p_copy(n).start()
 
-        obuf[n] = o.T.astype(jnp.bfloat16)
+        obuf[n] = (o.T * gain[...]).astype(jnp.bfloat16)
 
         @pl.when(n != y)
         def _():
@@ -258,6 +260,8 @@
             return 0
 
         lax.fori_loop(1, 4, relay, 0)
+        for a in range(2):
+            own_copy(a, fwd_send.at[a, 0], sibling).start()
 
         def from_sibling(j, _):
             slot = ((y + across(j)) % 4) * 2 + 1 - core
@@ -307,8 +311,8 @@
         turn(mine)
         for d in (1, 3, 2):
             q_copy(d).wait_send()
-        for d in (1, 3):
-            for a in range(2):
+        for a in range(2):
+            for d in (1, 3):
                 kv_copy(a, d).start()
         forward(1, 0)
         for d in (1, 3, 2):
@@ -380,14 +384,13 @@
     square[...] = total
 
     def s_copy(d):
-        return remote(square, squares.at[tp], s_send.at[d], s_recv.at[16 - d], (mine, (tp + d) % 16))
+        return remote(square, squares.at[15 - d], s_send.at[0], s_recv.at[0], (mine, (tp + d) % 16))
 
     for d in range(1, 16):
         s_copy(d).start()
-    for d in range(1, 16):
-        other = (tp + d) % 16
-        remote(square, squares.at[other], s_send.at[d], s_recv.at[d], sibling).wait_recv()
-        total = total + squares[other]
+    all_sums = remote(squares, squares, s_send.at[0], s_recv.at[0], sibling)
+    all_sums.wait_recv()
+    total = total + jnp.sum(squares[...], axis=0)
     factor_ref[...] = lax.rsqrt(total * (1.0 / D) + EPSILON)
 
     own.wait()
@@ -401,8 +404,9 @@
         def _():
             q_copy(d).wait_send()
     for d in range(1, 16):
-        s_copy(d).wait_send()
         doc_copy(d).wait_send()
+
+    all_sums.wait_send()
 
     def sent(v, _):
         for a in range(2):
@@ -422,7 +426,7 @@
             kv_copy(a, 2).wait_send()
 
 
-def fused(queries, keys, values, docs):
+def fused(queries, keys, values, docs, gain):
     hbm = pl.BlockSpec(memory_space=pltpu.HBM)
     vmem = pl.BlockSpec(memory_space=pltpu.VMEM)
     dma = pltpu.SemaphoreType.DMA
@@ -434,9 +438,10 @@
             jax.ShapeDtypeStruct((CHUNK, 4 * HEAD_DIM), bf16),
             jax.ShapeDtypeStruct((1, CHUNK), f32),
         ],
-        in_specs=[hbm] * 4,
+        in_specs=[hbm] * 5,
         out_specs=[vmem] * 2,
         scratch_shapes=[
+            pltpu.VMEM((1, HEAD_DIM), f32),
             pltpu.VMEM((4, CHUNK, HEAD_DIM), bf16),
             pltpu.VMEM((16, CHUNK, HEAD_DIM), bf16),
             pltpu.VMEM((16, CHUNK, HEAD_DIM), bf16),
@@ -451,18 +456,19 @@
             pltpu.VMEM((4, 1, CHUNK), f32),
             pltpu.VMEM((4, 1, CHUNK), f32),
             pltpu.VMEM((1, CHUNK), f32),
-            pltpu.VMEM((16, 1, CHUNK), f32),
-            dma((4,)), dma((4,)), dma((2, 4)), dma((2, 16)), dma((2, 8)), dma((2, 4)), dma((16,)), dma((16,)), dma((5,)),
+            pltpu.VMEM((15, 1, CHUNK), f32),
+            dma((4,)), dma((4,)), dma((2, 4)), dma((2, 16)), dma((2, 8)), dma((2, 4)), dma((16,)), dma((16,)), dma((6,)),
             dma((4,)), dma((4,)), dma((4,)), dma((4,)), dma((16,)), dma((16,)),
         ],
         compiler_params=pltpu.CompilerParams(collective_id=0, has_side_effects=True, vmem_limit_bytes=56 * 10**6),
-    )(queries, keys, values, docs)
+    )(queries, keys, values, docs, gain)
 
 
 def local(queries, keys, values, doc_ids, attn_gain):
-    rows, factor = fused(queries, keys, values, doc_ids.reshape(4, 128))
-    blended = attn_gain[None, :] * rows.astype(jnp.float32) * factor.reshape(CHUNK, 1)
-    return blended.astype(jnp.bfloat16)
+    docs, gain = doc_ids.reshape(4, 128), attn_gain.reshape(1, 4 * HEAD_DIM)
+    docs, gain = (pltpu.with_memory_space_constraint(x, pltpu.HBM) for x in (docs, gain))
+    rows, factor = fused(queries, keys, values, docs, gain)
+    return (rows.astype(jnp.float32) * factor.reshape(CHUNK, 1)).astype(jnp.bfloat16)
 
 
 def solution(mesh):

time: 56.2 us -> 55.2 us (0.982)
  local copies, waits for them, and re-layouts: 1.36 us -> 0 us
    unnamed x4 -> x0, local copies, waits for them, and re-layouts: 1.36 us -> none
where the time goes in v5:
time: 55.2 us
  Pallas kernels  54.2 us (98%)
  other arithmetic  0.96 us (2%)
    pallas_call x1, Pallas kernels, fused(): pl.pallas_call(fused_kernel, name='fused', out_shape=[jax.ShapeDtypeStruc...  54.2 us

profile of v5, /device:TPU:4, one launch (start us, length us, event | category | flops | bytes accessed | tf_op | source)
XLA Modules:
  0.0 55.2 jit_solution(16922183970539373496)
XLA Ops:
  0.0 54.2 %fused.1 = (bf16[512,512]{1,0:T(8,128)(2,1)S(1)}, f32[1,512]{1,0:T(1,128)S(1)}) custom-call(bf16[512,512]{1,0:T(8,128)(2,1)} %q_ref.1, bf16[512,512]{1,0:T(8,128)(2,1)} %k_ref.1, bf16[512,512]{1,0:T(8,128)(2,1)} %v_ref.1, s32[4,128]{1,0:T(4,128)} %bitcast.4, f32[1,512]{1,0:T(1,128)} %bitcast.5), custom_call_target="tpu_custom_call" | custom-call | tf_op jit(solution)/shard_map/fused/pallas_call | solution.py:434
  54.2 1.0 %multiply_convert_fusion = bf16[512,512]{1,0:T(8,128)(2,1)} fusion(bf16[512,512]{1,0:T(8,128)(2,1)S(1)} %get-tuple-element.7, f32[512]{0:T(512)S(1)} %bitcast.3), kind=kLoop, calls=%fused_computation | loop fusion | flops 786432 | bytes 1050624 | tf_op jit(solution)/shard_map/convert_element_type | solution.py:471

commit v6 on v5

--- a/solution.py
+++ b/solution.py
@@ -327,6 +327,14 @@
             final = v == 7
 
             def ahead():
+                @pl.when(v == 1)
+                def _():
+                    for d in (1, 3):
+                        for a in range(2):
+                            kv_copy(a, d).wait_send()
+                    for a in range(2):
+                        kv_copy(a, 2).start()
+
                 for at_visit, low, high in ((1, 2, 4), (2, 4, 5), (4, 5, 6), (5, 6, 7), (6, 7, 8)):
                     @pl.when(v == at_visit)
                     def _():
@@ -335,14 +343,6 @@
             @pl.when(final)
             def _():
                 lax.fori_loop(count, 4, finish, 0)
-
-            @pl.when(v == 2)
-            def _():
-                for d in (1, 3):
-                    for a in range(2):
-                        kv_copy(a, d).wait_send()
-                for a in range(2):
-                    kv_copy(a, 2).start()
 
             landed(slot_b)
             turn(slot_b)

time: 55.2 us -> 54.4 us (0.986)
  Pallas kernels: 54.2 us -> 53.4 us
    pallas_call x1, Pallas kernels: 54.2 us -> 53.4 us  [fused(): pl.pallas_call(fused_kernel, name='fused', out_shape=[jax.ShapeDtypeStruc...]
where the time goes in v6:
time: 54.4 us; the launch traced here: 54.3 us
  Pallas kernels  53.4 us (98%)
  other arithmetic  0.96 us (2%)
    pallas_call x1, Pallas kernels, fused(): pl.pallas_call(fused_kernel, name='fused', out_shape=[jax.ShapeDtypeStruc...  53.4 us

profile of v6, /device:TPU:4, one launch (start us, length us, event | category | flops | bytes accessed | tf_op | source)
XLA Modules:
  0.0 54.3 jit_solution(18345248951865474212)
XLA Ops:
  0.0 53.4 %fused.1 = (bf16[512,512]{1,0:T(8,128)(2,1)S(1)}, f32[1,512]{1,0:T(1,128)S(1)}) custom-call(bf16[512,512]{1,0:T(8,128)(2,1)} %q_ref.1, bf16[512,512]{1,0:T(8,128)(2,1)} %k_ref.1, bf16[512,512]{1,0:T(8,128)(2,1)} %v_ref.1, s32[4,128]{1,0:T(4,128)} %bitcast.4, f32[1,512]{1,0:T(1,128)} %bitcast.5), custom_call_target="tpu_custom_call" | custom-call | tf_op jit(solution)/shard_map/fused/pallas_call | solution.py:434
  53.4 1.0 %multiply_convert_fusion = bf16[512,512]{1,0:T(8,128)(2,1)} fusion(bf16[512,512]{1,0:T(8,128)(2,1)S(1)} %get-tuple-element.7, f32[512]{0:T(512)S(1)} %bitcast.3), kind=kLoop, calls=%fused_computation | loop fusion | flops 786432 | bytes 1050624 | tf_op jit(solution)/shard_map/convert_element_type | solution.py:471
